TPU v7x, 32 devices: a whole 2x2x4 slice. The times are simulated.
32 devices in a mesh: seq: 8 (over z, core), mp: 4 (over y, x).
Axes of the slice: x: 2, y: 2, z: 4, core: 2. Of those that a mesh axis runs over, the one named last changes fastest.
Arguments:
- tokens_in: bfloat16 [16384, 2048], P('seq'), may hold values from -6 to 6
- norm_gain: float32 [2048], replicated, may hold values from 0.5 to 200
- q_weight: bfloat16 [2048, 2048], P('seq', 'mp'), may hold values from -0.125 to 0.125
- kv_weight: bfloat16 [4, 2048, 128], P(None, 'seq'), may hold values from -0.125 to 0.125
- out_weight: bfloat16 [2048, 2048], P('seq', 'mp'), may hold values from -0.25 to 0.25
- segment_ids: int32 [16384], P('seq'), may hold values from 0 to 15, never falling along the last dimension, each value on 1 to 4096 neighbouring positions
- page_table: int32 [128], P('seq'), may hold values from 0 to 127, as said below
Outputs:
- layer_out: bfloat16 [16384, 2048], P('seq', 'mp')
- kv_cache: bfloat16 [128, 512, 128], P('seq', 'mp')
Inputs may be any that keep to these rules, and one draw needn't show every extreme that they name: `segment_ids`: segment numbers never fall along the stream; each of the 16 segments holds 1 to 4096 tokens and one holds exactly 4096. `page_table`: A permutation of the 128 cache slots; slot s belongs to index s // 16 of seq. The pages of index i of seq go to the indices i + o, counted round, for 8 distinct offsets o that are the same for every i, among them 1 and 8 / 2; exactly 2 pages to each owner.
All inputs are finite; a program needn't handle non-finite values.
Results may differ from a plain program's by a relative error of at most 0.018.
The roundings to bfloat16 on the way count: a program that leaves them out, or rounds other values in their place, can miss the bound.
Values may be sent and summed in bfloat16 or wider, within the bound.
A program may use at most 128 MiB of HBM per device.

v0:
```python
import math

import jax
import jax.numpy as jnp
from jax import lax
from jax.sharding import PartitionSpec as P

W = 2048
PAGE = 128


def prefix(value, axis, join, neutral):
    count, mine = (lax.axis_size(axis), lax.axis_index(axis))
    pieces = jax.tree.map(lambda part: lax.all_gather(part, axis), value)
    so_far = jax.tree.map(
        lambda part, zero: jnp.full_like(part, 0) + jnp.asarray(zero, part.dtype), value, neutral
    )

    def hop(position, so_far):
        longer = join(so_far, jax.tree.map(lambda part: part[position], pieces))
        return jax.tree.map(lambda new, old: jnp.where(position < mine, new, old), longer, so_far)

    return lax.fori_loop(0, count - 1, hop, so_far)


def from_behind(x, axis, by):
    peers = lax.axis_size(axis)
    pairs = [(i, i + by) for i in range(peers) if 0 <= i + by < peers]
    return lax.ppermute(x, axis, pairs)


def rotate_half(values, cosine, sine_table):
    half = values.shape[-1] // 2
    first_half = values[..., :half]
    second = values[..., half:]
    return jnp.concatenate(
        [first_half * cosine - second * sine_table, second * cosine + first_half * sine_table],
        axis=-1,
    )


def link_segments(earlier, later):
    seg_early, start_early = earlier
    seg_late, start_late = later
    merged_seg = jnp.maximum(seg_early, seg_late)
    merged_start = jnp.where(
        seg_late > seg_early,
        start_late,
        jnp.where(seg_early > seg_late, start_early, jnp.minimum(start_early, start_late)),
    )
    return (merged_seg, merged_start)


def attend_piece(carry, piece, start, queries, query_first, query_start, block_rows):
    head_size = queries.shape[2]
    count = piece.shape[0]
    key_rows = piece[:, :head_size]
    value_rows = piece[:, head_size:]
    key_index = start + jnp.arange(count, dtype=jnp.int32)
    scale = 1.0 / math.sqrt(head_size)
    blocks = queries.shape[0] // block_rows

    def one_block(block, state):
        row_first = block * block_rows
        query_block = lax.dynamic_slice_in_dim(queries, row_first, block_rows, 0)
        query_index = query_first + row_first + jnp.arange(block_rows, dtype=jnp.int32)
        query_begin = lax.dynamic_slice_in_dim(query_start, row_first, block_rows, 0)
        lowest = jnp.maximum(query_begin[0], query_index[0] - W + 1)
        live = (start <= query_index[-1]) & (start + count - 1 >= lowest)

        def compute(inner):
            best, totals, accum = inner
            best_block = lax.dynamic_slice_in_dim(best, row_first, block_rows, 1)
            total_block = lax.dynamic_slice_in_dim(totals, row_first, block_rows, 1)
            accum_block = lax.dynamic_slice_in_dim(accum, row_first, block_rows, 1)
            scores = (
                jnp.einsum("qhd,kd->hqk", query_block, key_rows, preferred_element_type=jnp.float32)
                * scale
            )
            keep = (key_index[None, :] >= query_begin[:, None]) & (
                key_index[None, :] <= query_index[:, None]
            )
            keep = keep & (query_index[:, None] - key_index[None, :] < W)
            masked = jnp.where(keep[None], scores, -1e30)
            new_best = jnp.maximum(best_block, jnp.max(masked, axis=-1))
            weights = jnp.where(keep[None], jnp.exp(masked - new_best[..., None]), 0.0)
            factor = jnp.exp(best_block - new_best)
            new_total = total_block * factor + jnp.sum(weights, axis=-1)
            mixed = jnp.einsum(
                "hqk,kd->hqd",
                weights.astype(jnp.bfloat16),
                value_rows,
                preferred_element_type=jnp.float32,
            )
            new_accum = accum_block * factor[..., None] + mixed
            best = lax.dynamic_update_slice_in_dim(best, new_best, row_first, 1)
            totals = lax.dynamic_update_slice_in_dim(totals, new_total, row_first, 1)
            accum = lax.dynamic_update_slice_in_dim(accum, new_accum, row_first, 1)
            return (best, totals, accum)

        return lax.cond(live, compute, lambda inner: inner, state)

    return lax.fori_loop(0, blocks, one_block, carry)


def body(tokens_in, norm_gain, q_weight, kv_weight, out_weight, segment_ids, page_table):
    seq_count = lax.axis_size("seq")
    mp_count = lax.axis_size("mp")
    seq_index = lax.axis_index("seq")
    mp_index = lax.axis_index("mp")
    tok_rows = tokens_in.shape[0]
    kv_heads = kv_weight.shape[0]
    head_size = kv_weight.shape[2] // 2
    ratio = mp_count // kv_heads
    own_head = mp_index // ratio
    kv_own = lax.dynamic_index_in_dim(kv_weight, own_head, 0, keepdims=False)
    w_query, w_keyval, w_output = (
        lax.all_gather(q_weight, "seq", axis=0, tiled=True),
        lax.all_gather(kv_own, "seq", axis=0, tiled=True),
        lax.all_gather(out_weight, "seq", axis=0, tiled=True),
    )
    inputs = tokens_in.astype(jnp.float32)
    meansq = jnp.mean(inputs * inputs, axis=-1, keepdims=True)
    normed = (inputs * lax.rsqrt(meansq + 1e-05) * norm_gain).astype(jnp.bfloat16)
    token_first = seq_index * tok_rows
    global_index = token_first + jnp.arange(tok_rows, dtype=jnp.int32)
    boundary = jnp.concatenate([jnp.ones((1,), bool), segment_ids[1:] != segment_ids[:-1]])
    local_start = lax.cummax(jnp.where(boundary, global_index, jnp.int32(0)), axis=0)
    prior_seg, prior_start = prefix(
        (segment_ids[-1], local_start[-1]), "seq", link_segments, (jnp.int32(-1), jnp.int32(0))
    )
    query_start = jnp.where(segment_ids == prior_seg, prior_start, local_start)
    positions = global_index - query_start
    half = head_size // 2
    freqs = jnp.exp(jnp.arange(half, dtype=jnp.float32) * (-2.0 * math.log(10000.0) / head_size))
    angles = positions.astype(jnp.float32)[:, None] * freqs[None, :]
    cosine = jnp.cos(angles)
    sine_table = jnp.sin(angles)
    local_heads = w_query.shape[1] // head_size
    queries = jnp.dot(normed, w_query, preferred_element_type=jnp.float32).reshape(
        tok_rows, local_heads, head_size
    )
    queries = rotate_half(queries, cosine[:, None, :], sine_table[:, None, :]).astype(jnp.bfloat16)
    projected = jnp.dot(normed, w_keyval, preferred_element_type=jnp.float32)
    key_rows = rotate_half(projected[:, :head_size], cosine, sine_table).astype(jnp.bfloat16)
    value_rows = projected[:, head_size:].astype(jnp.bfloat16)
    keyval = jnp.concatenate([key_rows, value_rows], axis=1)
    block_rows = min(512, tok_rows)
    initial = (
        jnp.full((local_heads, tok_rows), -1e30, jnp.float32),
        jnp.zeros((local_heads, tok_rows), jnp.float32),
        jnp.zeros((local_heads, tok_rows, head_size), jnp.float32),
    )

    def fold_piece(carry, piece, start):
        return attend_piece(carry, piece, start, queries, token_first, query_start, block_rows)

    state = fold_piece(initial, keyval, token_first)
    earlier = from_behind(keyval, "seq", 1)
    state = fold_piece(state, earlier, token_first - tok_rows)
    best, totals, accum = state
    attended = (
        (accum / totals[..., None])
        .transpose(1, 0, 2)
        .reshape(tok_rows, local_heads * head_size)
        .astype(jnp.bfloat16)
    )
    partial_term = lax.dot_general(
        attended, w_output, (((1,), (1,)), ((), ())), preferred_element_type=jnp.float32
    )
    layer_out = lax.psum_scatter(
        partial_term.astype(jnp.bfloat16), "mp", scatter_dimension=1, tiled=True
    )
    pages_dev = tok_rows // PAGE
    share_width = 2 * head_size // ratio
    share_index = mp_index % ratio
    share = lax.dynamic_slice_in_dim(keyval, share_index * share_width, share_width, 1)
    page_blocks = share.reshape(pages_dev, PAGE, share_width).transpose(0, 2, 1)
    owners = page_table // pages_dev
    local_slot = page_table % pages_dev
    spread = min(seq_count, pages_dev)
    capacity = pages_dev // spread
    page_order = jnp.arange(pages_dev, dtype=jnp.int32)
    same_owner = (owners[:, None] == owners[None, :]) & (page_order[None, :] < page_order[:, None])
    ranking = jnp.sum(same_owner.astype(jnp.int32), axis=1)
    send_lane = owners * capacity + ranking
    lanes_all = seq_count * capacity
    select = jnp.arange(lanes_all, dtype=jnp.int32)[:, None] == send_lane[None, :]
    outgoing = jnp.einsum(
        "sp,pfk->sfk", select.astype(jnp.bfloat16), page_blocks, preferred_element_type=jnp.float32
    ).astype(jnp.bfloat16)
    outgoing = outgoing.reshape(seq_count, capacity, share_width, PAGE)
    labels = (
        jnp.dot(select.astype(jnp.float32), (local_slot + 1).astype(jnp.float32))
        .astype(jnp.bfloat16)
        .reshape(seq_count, capacity)
    )
    incoming, tags = (
        lax.all_to_all(outgoing, "seq", split_axis=0, concat_axis=0, tiled=True),
        lax.all_to_all(labels, "seq", split_axis=0, concat_axis=0, tiled=True),
    )
    tags_flat = tags.reshape(lanes_all).astype(jnp.float32)
    placement = (tags_flat[None, :] == (page_order + 1).astype(jnp.float32)[:, None]).astype(
        jnp.bfloat16
    )
    kv_cache = jnp.einsum(
        "ps,sfk->pfk",
        placement,
        incoming.reshape(lanes_all, share_width, PAGE),
        preferred_element_type=jnp.float32,
    ).astype(jnp.bfloat16)
    return (layer_out, kv_cache)


def solution(mesh):
    placed = (
        P("seq", None),
        P(),
        P("seq", "mp"),
        P(None, "seq", None),
        P("seq", "mp"),
        P("seq"),
        P("seq"),
    )
    return jax.shard_map(
        body,
        mesh=mesh,
        in_specs=placed,
        out_specs=(P("seq", "mp"), P("seq", "mp", None)),
        check_vma=False,
    )
```

profile of v0, /device:TPU:0, one launch (start us, length us, event | category | flops | bytes accessed | tf_op | source)
XLA Modules:
  0.0 617.3 jit_solution(7080078336438234559)
XLA Ops:
  13.0 10.7 %all-reduce.2 = (s32[8]{0:T(128)S(1)}, s32[8]{0:T(128)S(1)}) all-reduce(s32[8]{0:T(128)S(1)} %slice_dynamic-update-slice_fusion.1, s32[8]{0:T(128)S(1)} %slice_dynamic-update-slice_fusion), channel_id=1, replica_groups=mesh['seq'=8,'mp'=4] {'seq'}, use_global_device_ids=true, to_apply=%add | all-reduce | flops 16 | bytes 128
  23.8 5.3 fusion.50
  29.1 16.9 %all-gather = bf16[1,2048,128]{2,1,0:T(8,128)(2,1)S(1)} all-gather(bf16[1,256,128]{2,1,0:T(8,128)(2,1)S(1)} %constant_dynamic-slice_fusion), channel_id=2, replica_groups=mesh['seq'=8,'mp'=4] {'seq'}, dimensions={1}, use_global_device_ids=true | all-gather | bytes 589824 | tf_op jit(solution)/shard_map/all_gather | solution.py:119
  48.8 29.3 %while.61 = (s32[]{:T(128)}, s32[]{:T(128)}, s32[]{:T(128)}, s32[]{:T(128)}, s32[8]{0:T(128)S(1)}, /*index=5*/s32[8]{0:T(128)S(1)}, s32[]{:T(128)}) while((s32[]{:T(128)}, s32[]{:T(128)}, s32[]{:T(128)}, s32[]{:T(128)}, s32[8]{0:T(128)S(1)}, /*index=5*/s32[8]{0:T(128)S(1)}, s32[]{:T(128)}) %tuple.189), condition=%wide.region_4.5_spmd, body=%wide.region_3.4_spmd.sunk | while | flops 11 | bytes 220 | solution.py:23
  85.0 7.9 %fusion.55 = f32[2048,512]{0,1:T(8,128)S(1)} fusion(bf16[2048,512]{1,0:T(8,128)(2,1)} %all-gather.4.cloned.1.call-done, bf16[2048,2048]{1,0:T(8,128)(2,1)} %param.17, f32[2048]{0:T(1024)S(1)} %copy-done.7, f32[2048]{0:T(1024)S(1)} %add_rsqrt_fusion), kind=kOutput, calls=%fused_computation.66 | convolution fusion | flops 4311744512 | bytes 14696448 | tf_op jit(solution)/shard_map/dot_general | solution.py:140
  96.3 205.8 %while.62 = (s32[]{:T(128)}, f32[8,2048]{1,0:T(8,128)S(1)}, f32[8,2048]{1,0:T(8,128)S(1)}, f32[8,2048,64]{1,2,0:T(8,128)}, s32[]{:T(128)}, /*index=5*/s32[2048]{...) while((s32[]{:T(128)}, f32[8,2048]{1,0:T(8,128)S(1)}, ...), condition=%wide.region_10.11_spmd.clone.clone, body=%wide.region_5.10_spmd.clone.clone.sunk | while | flops 2263362048 | bytes 109603304 | solution.py:103
  99.5 48.2 %conditional.8 = ((f32[8,2048]{1,0:T(8,128)S(1)}, f32[8,2048]{1,0:T(8,128)S(1)}, f32[8,2048,64]{1,2,0:T(8,128)})) conditional(s32[]{:T(128)} %convert_element_type.153, (f32[8,2048]{1,0:T(8,128)S(1)}, f32[8,2048]{1,0:T(8,128)S(1)}, f32[8,2048,64]{1,2,0:T(8,128)}) %tuple.179, (s32[]{:T(128)}, f32[8,2048]{1,0:T(8,128)S(1)}, s32[]{:T(128)}, ...), branch_computations={%region_6.6_spmd, %region_7.9_spmd} | conditional | flops 2263361536 | bytes 109588560 | solution.py:101
  99.6 2.9 fusion.12
  102.5 13.7 %bitcast_reduce_fusion = (f32[8,512]{1,0:T(8,128)S(1)}, f32[512,8,2048]{2,0,1:T(8,128)}) fusion(pred[512,2048]{1,0:T(8,128)(4,1)S(1)} %fusion.12, bf16[2048,64]{0,1:T(8,128)(2,1)S(1)} %get-tuple-element.929, bf16[2048,8,64]{0,2,1:T(8,128)(2,1)S(1)} %get-tuple-element.927, s32[]{:T(128)} %get-tuple-element.928), kind=kOutput, calls=%fused_computation.3 | convolution fusion | flops 1098903552 | bytes 35405828 | tf_op jit(solution)/shard_map/while/body/eval_jaxpr/cond/branch_1_fun/qhd,kd->hqk/dot_general | solution.py:77
  116.2 15.6 %fusion.7 = f32[8,512]{1,0:T(8,128)S(1)} fusion(f32[512,8,2048]{2,0,1:T(8,128)} %get-tuple-element.1186, f32[8,512]{1,0:T(8,128)S(1)} %get-tuple-element.1178, pred[512,2048]{1,0:T(8,128)(4,1)S(1)} %fusion.12), kind=kLoop, calls=%fused_computation.8 | loop fusion | flops 41938944 | bytes 34635776 | tf_op jit(solution)/shard_map/while/body/eval_jaxpr/cond/branch_1_fun/reduce_sum | solution.py:88
  131.8 15.9 %fusion.16 = f32[8,2048,64]{1,2,0:T(8,128)} fusion(f32[8,2048,64]{1,2,0:T(8,128)} %get-tuple-element.931, s32[]{:T(128)S(6)} %select_n.120, f32[512,8,2048]{2,0,1:T(8,128)} %get-tuple-element.1186, f32[8,512]{1,0:T(8,128)S(1)} %get-tuple-element.1178, pred[512,2048]{1,0:T(8,128)(4,1)S(1)} %fusion.12, f32[8,512]{1,0:T(8,128)S(1)} %get-tuple-element.1176, ...), kind=kOutput, calls=%fused_computation.15 | convolution fusion | flops 1116209152 | bytes 38043652 | tf_op jit(solution)/shard_map/while/body/eval_jaxpr/cond/branch_1_fun/hqk,kd->hqd/dot_general | solution.py:89
  150.9 48.4 %conditional.8 = ((f32[8,2048]{1,0:T(8,128)S(1)}, f32[8,2048]{1,0:T(8,128)S(1)}, f32[8,2048,64]{1,2,0:T(8,128)})) conditional(s32[]{:T(128)} %convert_element_type.153, (f32[8,2048]{1,0:T(8,128)S(1)}, f32[8,2048]{1,0:T(8,128)S(1)}, f32[8,2048,64]{1,2,0:T(8,128)}) %tuple.179, (s32[]{:T(128)}, f32[8,2048]{1,0:T(8,128)S(1)}, s32[]{:T(128)}, ...), branch_computations={%region_6.6_spmd, %region_7.9_spmd} | conditional | flops 2263361536 | bytes 109588560 | solution.py:101
  151.0 2.9 fusion.12
  153.8 13.7 %bitcast_reduce_fusion = (f32[8,512]{1,0:T(8,128)S(1)}, f32[512,8,2048]{2,0,1:T(8,128)}) fusion(pred[512,2048]{1,0:T(8,128)(4,1)S(1)} %fusion.12, bf16[2048,64]{0,1:T(8,128)(2,1)S(1)} %get-tuple-element.929, bf16[2048,8,64]{0,2,1:T(8,128)(2,1)S(1)} %get-tuple-element.927, s32[]{:T(128)} %get-tuple-element.928), kind=kOutput, calls=%fused_computation.3 | convolution fusion | flops 1098903552 | bytes 35405828 | tf_op jit(solution)/shard_map/while/body/eval_jaxpr/cond/branch_1_fun/qhd,kd->hqk/dot_general | solution.py:77
  167.5 15.6 %fusion.7 = f32[8,512]{1,0:T(8,128)S(1)} fusion(f32[512,8,2048]{2,0,1:T(8,128)} %get-tuple-element.1186, f32[8,512]{1,0:T(8,128)S(1)} %get-tuple-element.1178, pred[512,2048]{1,0:T(8,128)(4,1)S(1)} %fusion.12), kind=kLoop, calls=%fused_computation.8 | loop fusion | flops 41938944 | bytes 34635776 | tf_op jit(solution)/shard_map/while/body/eval_jaxpr/cond/branch_1_fun/reduce_sum | solution.py:88
  183.1 16.1 %fusion.16 = f32[8,2048,64]{1,2,0:T(8,128)} fusion(f32[8,2048,64]{1,2,0:T(8,128)} %get-tuple-element.931, s32[]{:T(128)S(6)} %select_n.120, f32[512,8,2048]{2,0,1:T(8,128)} %get-tuple-element.1186, f32[8,512]{1,0:T(8,128)S(1)} %get-tuple-element.1178, pred[512,2048]{1,0:T(8,128)(4,1)S(1)} %fusion.12, f32[8,512]{1,0:T(8,128)S(1)} %get-tuple-element.1176, ...), kind=kOutput, calls=%fused_computation.15 | convolution fusion | flops 1116209152 | bytes 38043652 | tf_op jit(solution)/shard_map/while/body/eval_jaxpr/cond/branch_1_fun/hqk,kd->hqd/dot_general | solution.py:89
  202.5 48.2 %conditional.8 = ((f32[8,2048]{1,0:T(8,128)S(1)}, f32[8,2048]{1,0:T(8,128)S(1)}, f32[8,2048,64]{1,2,0:T(8,128)})) conditional(s32[]{:T(128)} %convert_element_type.153, (f32[8,2048]{1,0:T(8,128)S(1)}, f32[8,2048]{1,0:T(8,128)S(1)}, f32[8,2048,64]{1,2,0:T(8,128)}) %tuple.179, (s32[]{:T(128)}, f32[8,2048]{1,0:T(8,128)S(1)}, s32[]{:T(128)}, ...), branch_computations={%region_6.6_spmd, %region_7.9_spmd} | conditional | flops 2263361536 | bytes 109588560 | solution.py:101
  202.5 2.9 fusion.12
  205.4 13.7 %bitcast_reduce_fusion = (f32[8,512]{1,0:T(8,128)S(1)}, f32[512,8,2048]{2,0,1:T(8,128)}) fusion(pred[512,2048]{1,0:T(8,128)(4,1)S(1)} %fusion.12, bf16[2048,64]{0,1:T(8,128)(2,1)S(1)} %get-tuple-element.929, bf16[2048,8,64]{0,2,1:T(8,128)(2,1)S(1)} %get-tuple-element.927, s32[]{:T(128)} %get-tuple-element.928), kind=kOutput, calls=%fused_computation.3 | convolution fusion | flops 1098903552 | bytes 35405828 | tf_op jit(solution)/shard_map/while/body/eval_jaxpr/cond/branch_1_fun/qhd,kd->hqk/dot_general | solution.py:77
  219.1 15.6 %fusion.7 = f32[8,512]{1,0:T(8,128)S(1)} fusion(f32[512,8,2048]{2,0,1:T(8,128)} %get-tuple-element.1186, f32[8,512]{1,0:T(8,128)S(1)} %get-tuple-element.1178, pred[512,2048]{1,0:T(8,128)(4,1)S(1)} %fusion.12), kind=kLoop, calls=%fused_computation.8 | loop fusion | flops 41938944 | bytes 34635776 | tf_op jit(solution)/shard_map/while/body/eval_jaxpr/cond/branch_1_fun/reduce_sum | solution.py:88
  234.7 16.0 %fusion.16 = f32[8,2048,64]{1,2,0:T(8,128)} fusion(f32[8,2048,64]{1,2,0:T(8,128)} %get-tuple-element.931, s32[]{:T(128)S(6)} %select_n.120, f32[512,8,2048]{2,0,1:T(8,128)} %get-tuple-element.1186, f32[8,512]{1,0:T(8,128)S(1)} %get-tuple-element.1178, pred[512,2048]{1,0:T(8,128)(4,1)S(1)} %fusion.12, f32[8,512]{1,0:T(8,128)S(1)} %get-tuple-element.1176, ...), kind=kOutput, calls=%fused_computation.15 | convolution fusion | flops 1116209152 | bytes 38043652 | tf_op jit(solution)/shard_map/while/body/eval_jaxpr/cond/branch_1_fun/hqk,kd->hqd/dot_general | solution.py:89
  253.9 48.2 %conditional.8 = ((f32[8,2048]{1,0:T(8,128)S(1)}, f32[8,2048]{1,0:T(8,128)S(1)}, f32[8,2048,64]{1,2,0:T(8,128)})) conditional(s32[]{:T(128)} %convert_element_type.153, (f32[8,2048]{1,0:T(8,128)S(1)}, f32[8,2048]{1,0:T(8,128)S(1)}, f32[8,2048,64]{1,2,0:T(8,128)}) %tuple.179, (s32[]{:T(128)}, f32[8,2048]{1,0:T(8,128)S(1)}, s32[]{:T(128)}, ...), branch_computations={%region_6.6_spmd, %region_7.9_spmd} | conditional | flops 2263361536 | bytes 109588560 | solution.py:101
  256.8 13.7 %bitcast_reduce_fusion = (f32[8,512]{1,0:T(8,128)S(1)}, f32[512,8,2048]{2,0,1:T(8,128)}) fusion(pred[512,2048]{1,0:T(8,128)(4,1)S(1)} %fusion.12, bf16[2048,64]{0,1:T(8,128)(2,1)S(1)} %get-tuple-element.929, bf16[2048,8,64]{0,2,1:T(8,128)(2,1)S(1)} %get-tuple-element.927, s32[]{:T(128)} %get-tuple-element.928), kind=kOutput, calls=%fused_computation.3 | convolution fusion | flops 1098903552 | bytes 35405828 | tf_op jit(solution)/shard_map/while/body/eval_jaxpr/cond/branch_1_fun/qhd,kd->hqk/dot_general | solution.py:77
  270.5 15.6 %fusion.7 = f32[8,512]{1,0:T(8,128)S(1)} fusion(f32[512,8,2048]{2,0,1:T(8,128)} %get-tuple-element.1186, f32[8,512]{1,0:T(8,128)S(1)} %get-tuple-element.1178, pred[512,2048]{1,0:T(8,128)(4,1)S(1)} %fusion.12), kind=kLoop, calls=%fused_computation.8 | loop fusion | flops 41938944 | bytes 34635776 | tf_op jit(solution)/shard_map/while/body/eval_jaxpr/cond/branch_1_fun/reduce_sum | solution.py:88
  286.1 16.0 %fusion.16 = f32[8,2048,64]{1,2,0:T(8,128)} fusion(f32[8,2048,64]{1,2,0:T(8,128)} %get-tuple-element.931, s32[]{:T(128)S(6)} %select_n.120, f32[512,8,2048]{2,0,1:T(8,128)} %get-tuple-element.1186, f32[8,512]{1,0:T(8,128)S(1)} %get-tuple-element.1178, pred[512,2048]{1,0:T(8,128)(4,1)S(1)} %fusion.12, f32[8,512]{1,0:T(8,128)S(1)} %get-tuple-element.1176, ...), kind=kOutput, calls=%fused_computation.15 | convolution fusion | flops 1116209152 | bytes 38043652 | tf_op jit(solution)/shard_map/while/body/eval_jaxpr/cond/branch_1_fun/hqk,kd->hqd/dot_general | solution.py:89
  302.1 13.0 %while.63 = (s32[]{:T(128)}, f32[8,2048]{1,0:T(8,128)S(1)}, f32[8,2048]{1,0:T(8,128)S(1)}, f32[8,2048,64]{1,2,0:T(8,128)}, s32[]{:T(128)}, /*index=5*/s32[]{:T(1...) while((s32[]{:T(128)}, f32[8,2048]{1,0:T(8,128)S(1)}, ...), condition=%wide.region_16.17_spmd.clone.clone, body=%wide.region_11.16_spmd.clone.clone.sunk | while | flops 2263362048 | bytes 109603312 | solution.py:103
  317.8 8.7 %convolution_convert_fusion = bf16[2048,2048]{1,0:T(8,128)(2,1)} fusion(bf16[2048,512]{0,1:T(8,128)(2,1)S(1)} %bitcast.108, bf16[2048,512]{1,0:T(8,128)(2,1)} %all-gather.6.cloned.1.call-done), kind=kOutput, calls=%fused_computation.63 | convolution fusion | flops 4299161600 | bytes 12582912 | tf_op jit(solution)/shard_map/dot_general | solution.py:168
  328.1 201.4 %all-to-all-start = ((bf16[8,1,2]{2,1,0:T(2,128)(2,1)}), bf16[8,1,2]{2,1,0:T(2,128)(2,1)S(1)}, u32[]{:S(2)}, u32[]{:S(2)}) async-start(bf16[8,1,2]{2,1,0:T(2,128)(2,1)} %all_to_all.12), calls=%async_computation.1 | async-start | bytes 8192 | tf_op jit(solution)/shard_map/all_to_all | solution.py:200
  531.2 3.9 all-to-all-done
  535.1 3.5 all-to-all-start.1
  538.7 15.2 %all-to-all-done.1 = bf16[8,2,128,128]{3,1,2,0:T(2,128)(2,1)S(1)} async-done(((bf16[8,2,128,128]{3,1,2,0:T(2,128)(2,1)}), bf16[8,2,128,128]{3,1,2,0:T(2,128)(2,1)S(1)}, u32[]{:S(2)}, u32[]{:S(2)}) %all-to-all-start.1) | async-done | bytes 524320 | tf_op jit(solution)/shard_map/all_to_all | solution.py:199
  555.6 55.2 %reduce-scatter.2.cloned.1.call-done = bf16[2048,512]{1,0:T(8,128)(2,1)} async-done(((bf16[2048,2048]{1,0:T(8,128)(2,1)}), bf16[2048,512]{1,0:T(8,128)(2,1)}) %reduce-scatter.2.cloned.1.call-update) | async-done | bytes 2097168 | tf_op jit(solution)/shard_map/reduce_scatter | solution.py:171
  (149 shorter events, 48.2 us)
Async XLA Ops:
  7.2 16.6 %copy-start = (bf16[4,256,128]{2,1,0:T(8,128)(2,1)S(1)}, bf16[4,256,128]{2,1,0:T(8,128)(2,1)}, u32[]{:S(2)}) copy-start(bf16[4,256,128]{2,1,0:T(8,128)(2,1)} %param.20) | copy-start | bytes 786436
  7.2 38.8 %copy-start.7 = (f32[2048]{0:T(1024)S(1)}, f32[2048]{0:T(1024)}, u32[]{:S(2)}) copy-start(f32[2048]{0:T(1024)} %param.18) | copy-start | bytes 24580
  7.2 77.8 %all-gather.4.cloned.1.call-start = ((), (), s32[]{:S(2)}) async-start(), calls=%async_computation.3 | async-start | bytes 2359296 | tf_op jit(solution)/shard_map/all_gather | solution.py:118
  7.9 309.9 %all-gather.6.cloned.1.call-start = ((), (), s32[]{:S(2)}) async-start(), calls=%async_computation.4 | async-start | bytes 2359296 | tf_op jit(solution)/shard_map/all_gather | solution.py:120
  23.8 22.2 %copy-start.3 = (bf16[2048,2048]{1,0:T(8,128)(2,1)S(1)}, bf16[2048,2048]{1,0:T(8,128)(2,1)}, u32[]{:S(2)}) copy-start(bf16[2048,2048]{1,0:T(8,128)(2,1)} %param.17) | copy-start | bytes 25165828
  46.0 32.2 %copy-start.6 = (s32[2048]{0:T(1024)S(1)}, s32[2048]{0:T(1024)}, u32[]{:S(2)}) copy-start(s32[2048]{0:T(1024)} %param.22) | copy-start | bytes 24580
  80.4 3.8 collective-permute-start
  82.7 528.1 %reduce-scatter.2.cloned.1.call-start = ((), (), s32[]{:S(2)}) async-start(), calls=%async_computation.5 | async-start | bytes 10485760 | tf_op jit(solution)/shard_map/reduce_scatter | solution.py:171
  96.3 205.8 %copy-start.2 = (bf16[2048,64]{0,1:T(8,128)(2,1)S(1)}, bf16[2048,64]{0,1:T(8,128)(2,1)}, u32[]{:S(2)}) copy-start(bf16[2048,64]{0,1:T(8,128)(2,1)} %get-tuple-element.1475) | copy-start | bytes 786436
  96.3 205.8 %copy-start.5 = (bf16[2048,64]{0,1:T(8,128)(2,1)S(1)}, bf16[2048,64]{0,1:T(8,128)(2,1)}, u32[]{:S(2)}) copy-start(bf16[2048,64]{0,1:T(8,128)(2,1)} %get-tuple-element.1476) | copy-start | bytes 786436
  317.8 292.9 %copy-start.1 = (bf16[4,256,128]{2,1,0:T(8,128)(2,1)S(1)}, bf16[4,256,128]{2,1,0:T(8,128)(2,1)}, u32[]{:S(2)}) copy-start(bf16[4,256,128]{2,1,0:T(8,128)(2,1)} %param.20) | copy-start | bytes 786436
  326.5 0.7 copy-start.8
  326.5 203.1 %copy-start.4 = (bf16[16,8,16,128]{3,1,2,0:T(8,128)(2,1)S(1)}, bf16[16,8,16,128]{3,1,2,0:T(8,128)(2,1)}, u32[]{:S(2)}) copy-start(bf16[16,8,16,128]{3,1,2,0:T(8,128)(2,1)} %get-tuple-element.1197) | copy-start | bytes 1572868
  328.1 207.0 %all-to-all-start = ((bf16[8,1,2]{2,1,0:T(2,128)(2,1)}), bf16[8,1,2]{2,1,0:T(2,128)(2,1)S(1)}, u32[]{:S(2)}, u32[]{:S(2)}) async-start(bf16[8,1,2]{2,1,0:T(2,128)(2,1)} %all_to_all.12), calls=%async_computation.1 | async-start | bytes 8192 | tf_op jit(solution)/shard_map/all_to_all | solution.py:200
  535.1 18.8 %all-to-all-start.1 = ((bf16[8,2,128,128]{3,1,2,0:T(2,128)(2,1)}), bf16[8,2,128,128]{3,1,2,0:T(2,128)(2,1)S(1)}, u32[]{:S(2)}, u32[]{:S(2)}) async-start(bf16[8,2,128,128]{3,1,2,0:T(2,128)(2,1)} %copy.16), calls=%async_computation.2 | async-start | bytes 1048576 | tf_op jit(solution)/shard_map/all_to_all | solution.py:199
Sparse Core Ops, SparseCore 0:
  9.6 36.4 all-gather.3
  82.8 27.7 all-gather.5
  326.6 284.0 reduce-scatter.1
where the time goes:
time: 619 us; the launch traced here: 617 us
  starting transfers between devices  207 us (33%)
  matrix products  139 us (22%)
  other arithmetic  86.4 us (14%)
  waiting for transfers between devices  76.4 us (12%)
  loops' own time  36.9 us (6%)
  local copies, waits for them, and re-layouts  29.8 us (5%)
  blocking collectives  27.6 us (4%)
  between operations  14 us (2%)
    all_to_all x1, starting transfers between devices, body(): lax.all_to_all(labels, 'seq', split_axis=0, concat_axis=0, tiled=True)  201 us
    dot_general x4, matrix products, compute(): jnp.einsum('hqk,kd->hqd', weights.astype(jnp.bfloat16), value_rows, prefe...  64 us
    reduce_sum x4, other arithmetic, compute(): new_total = total_block * factor + jnp.sum(weights, axis=-1)  62.2 us
    reduce_scatter x1, waiting for transfers between devices, body(): lax.psum_scatter(partial_term.astype(jnp.bfloat16), 'mp', scatter_dimensi...  55.2 us
    dot_general x4, matrix products, compute(): jnp.einsum('qhd,kd->hqk', query_block, key_rows, preferred_element_type=j...  54.7 us
    another operation x1, loops' own time, prefix(): return lax.fori_loop(0, count - 1, hop, so_far)  21 us
    all_gather x1, blocking collectives, body(): lax.all_gather(kv_own, 'seq', axis=0, tiled=True)  16.9 us
    another operation x2, loops' own time, attend_piece(): return lax.fori_loop(0, blocks, one_block, carry)  15.6 us
  transfers between devices with their start and end apart: 6, of which 4 were waited for; matrix products, arithmetic and copies ran while one was open for 40% of the time, Pallas kernels for 0%

commit v1 on v0

v1 whole, which is shorter than its diff:
```python
import functools
import math

import jax
import jax.numpy as jnp
from jax import lax
from jax.experimental import pallas as pl
from jax.experimental.pallas import tpu as pltpu
from jax.sharding import PartitionSpec as P

W = 2048
PAGE = 128
BINS = 128
BQ = 256
BK = 768
CHUNKS = (512, 512, 512, 512)
LOG2E = 1.4426950408889634


def attend_kernel(heads, head_size, first, tok_rows, lows, low_ref, q_ref, k_ref, v_ref, o_ref,
                  q_scr, bias_scr, m_scr, acc_scr):
    block = pl.program_id(0)
    q0 = tok_rows + first + block * BQ
    end = q0 + BQ
    scale = LOG2E / math.sqrt(head_size)
    for h in range(heads):
        scaled = q_ref[h * head_size:(h + 1) * head_size, :].astype(jnp.float32) * scale
        high = scaled.astype(jnp.bfloat16)
        q_scr[h, :head_size, :] = high
        q_scr[h, head_size:, :] = (scaled - high.astype(jnp.float32)).astype(jnp.bfloat16)
    m_scr[...] = jnp.full_like(m_scr, -1e30)
    acc_scr[...] = jnp.zeros_like(acc_scr)
    low = low_ref[...]
    query = q0 + lax.broadcasted_iota(jnp.int32, (1, BQ), 1)
    steps = (end - lows[first // BQ + block] + BK - 1) // BK

    def step(j, carry):
        k0 = pl.multiple_of(end - (j + 1) * BK, 256)
        keys = k_ref[pl.ds(k0, BK), :]
        vals = v_ref[:, pl.ds(k0, BK)]
        key = k0 + lax.broadcasted_iota(jnp.int32, (BK, 1), 0)
        bias_scr[...] = jnp.where((key >= low) & (key <= query), 0.0, -1e30)

        def score(h):
            return jnp.dot(keys, q_scr[h], preferred_element_type=jnp.float32)

        s = score(0)
        for h in range(heads):
            following = score(h + 1) if h + 1 < heads else None
            s = s + bias_scr[...]
            old = m_scr[h]
            new = jnp.maximum(old, jnp.max(s, axis=0, keepdims=True))
            p = jnp.exp2(s - new).astype(jnp.bfloat16)
            mixed = jnp.dot(vals, p, preferred_element_type=jnp.float32)
            acc_scr[h] = acc_scr[h] * jnp.exp2(old - new) + mixed
            m_scr[h] = new
            s = following
        return carry

    lax.fori_loop(0, steps, step, 0)
    for h in range(heads):
        total = acc_scr[h, head_size:head_size + 1, :]
        o_ref[h * head_size:(h + 1) * head_size, :] = (
            acc_scr[h, :head_size, :] / total
        ).astype(jnp.bfloat16)


def attend(lows, low, q_t, keys, vals, first, count, heads, head_size):
    tok_rows = q_t.shape[1]
    off = first // BQ
    whole = lambda a: pl.BlockSpec(a.shape, lambda i, s: (0, 0))
    return pl.pallas_call(
        functools.partial(attend_kernel, heads, head_size, first, tok_rows),
        out_shape=jax.ShapeDtypeStruct((heads * head_size, count), jnp.bfloat16),
        grid_spec=pltpu.PrefetchScalarGridSpec(
            num_scalar_prefetch=1,
            grid=(count // BQ,),
            in_specs=[
                pl.BlockSpec((1, BQ), lambda i, s: (0, off + i)),
                pl.BlockSpec((heads * head_size, BQ), lambda i, s: (0, off + i)),
                whole(keys),
                whole(vals),
            ],
            out_specs=pl.BlockSpec((heads * head_size, BQ), lambda i, s: (0, i)),
            scratch_shapes=[
                pltpu.VMEM((heads, 2 * head_size, BQ), jnp.bfloat16),
                pltpu.VMEM((BK, BQ), jnp.float32),
                pltpu.VMEM((heads, 1, BQ), jnp.float32),
                pltpu.VMEM((heads, vals.shape[0], BQ), jnp.float32),
            ],
        ),
        compiler_params=pltpu.CompilerParams(vmem_limit_bytes=48 << 20),
        cost_estimate=pl.CostEstimate(
            flops=count * 2048 * heads * 256 * 2 * 2,
            bytes_accessed=6 << 20,
            transcendentals=count * 2304 * heads,
        ),
    )(lows, low, q_t, keys, vals)


def pick_kernel(pages, order, src, dst):
    for lane in range(pages):
        col = pl.multiple_of(order[lane] * PAGE, PAGE)
        dst[lane] = src[:, pl.ds(col, PAGE)]


def place_kernel(pages, order, src, dst):
    for slot in range(pages):
        dst[slot] = src[order[slot]]


def reorder(kernel, order, src, pages, rows):
    return pl.pallas_call(
        functools.partial(kernel, pages),
        out_shape=jax.ShapeDtypeStruct((pages, rows, PAGE), src.dtype),
        in_specs=[
            pl.BlockSpec(memory_space=pltpu.SMEM),
            pl.BlockSpec(memory_space=pltpu.VMEM),
        ],
        out_specs=pl.BlockSpec(memory_space=pltpu.VMEM),
        cost_estimate=pl.CostEstimate(flops=0, bytes_accessed=1 << 20, transcendentals=0),
    )(order, src)


def rotate(v, cosine, sine):
    half = v.shape[-2] // 2
    a, b = v[..., :half, :], v[..., half:, :]
    return jnp.concatenate([a * cosine - b * sine, b * cosine + a * sine], axis=-2)


def body(tokens_in, norm_gain, q_weight, kv_weight, out_weight, segment_ids, page_table):
    seq_count = lax.axis_size("seq")
    mp_count = lax.axis_size("mp")
    seq_index = lax.axis_index("seq")
    mp_index = lax.axis_index("mp")
    tok_rows = tokens_in.shape[0]
    kv_heads = kv_weight.shape[0]
    head_size = kv_weight.shape[2] // 2
    assert tok_rows == W
    ratio = mp_count // kv_heads
    share_width = 2 * head_size // ratio
    pages_dev = tok_rows // PAGE
    capacity = pages_dev // seq_count

    with jax.named_scope("gathers"):
        bins = jnp.arange(BINS, dtype=jnp.int32)
        below = jnp.sum((segment_ids[None, :] < bins[:, None]).astype(jnp.int32), axis=1)
        padded = jnp.pad(page_table, (0, BINS - pages_dev))
        info = lax.all_gather(jnp.stack([below, padded]), "seq")
        kv_own = lax.dynamic_index_in_dim(kv_weight, mp_index // ratio, 0, keepdims=False)
        w_keyval = lax.all_gather(kv_own, "seq", axis=0, tiled=True)
        w_query = lax.all_gather(q_weight, "seq", axis=0, tiled=True)
        late, w_query = lax.optimization_barrier((out_weight, w_query))
        w_output = lax.all_gather(late, "seq", axis=0, tiled=True)

    with jax.named_scope("norm"):
        inputs = tokens_in.astype(jnp.float32)
        meansq = jnp.mean(inputs * inputs, axis=-1, keepdims=True)
        normed = (inputs * lax.rsqrt(meansq + 1e-05) * norm_gain).astype(jnp.bfloat16)

    with jax.named_scope("positions"):
        starts = jnp.sum(info[:, 0, :], axis=0)
        one_hot = segment_ids[None, :] == bins[:, None]
        query_start = jnp.sum(jnp.where(one_hot, starts[:, None], 0), axis=0)
        token_first = seq_index * tok_rows
        local = jnp.arange(tok_rows, dtype=jnp.int32)
        positions = token_first + local - query_start
        half = head_size // 2
        freqs = jnp.exp(
            jnp.arange(half, dtype=jnp.float32) * (-2.0 * math.log(10000.0) / head_size)
        )
        angles = positions.astype(jnp.float32)[None, :] * freqs[:, None]
        cosine, sine = jnp.cos(angles), jnp.sin(angles)
        low = jnp.maximum(query_start - token_first + tok_rows, local + tok_rows - W + 1)
        lows = low[::BQ]

    with jax.named_scope("keyval"):
        kv_t = lax.dot_general(
            w_keyval, normed, (((0,), (1,)), ((), ())), preferred_element_type=jnp.float32
        )
        kv_t = jnp.concatenate(
            [rotate(kv_t[:head_size], cosine, sine), kv_t[head_size:]], axis=0
        ).astype(jnp.bfloat16)
        behind = lax.ppermute(kv_t, "seq", [(i, i + 1) for i in range(seq_count - 1)])

    with jax.named_scope("queries"):
        heads = w_query.shape[1] // head_size
        q_t = lax.dot_general(
            w_query, normed, (((0,), (1,)), ((), ())), preferred_element_type=jnp.float32
        ).reshape(heads, head_size, tok_rows)
        q_t = rotate(q_t, cosine, sine).astype(jnp.bfloat16).reshape(heads * head_size, tok_rows)

    with jax.named_scope("pages_out"):
        owners = page_table // pages_dev
        order = jnp.arange(pages_dev, dtype=jnp.int32)
        rank = jnp.sum(
            ((owners[:, None] == owners[None, :]) & (order[None, :] < order[:, None])).astype(
                jnp.int32
            ),
            axis=1,
        )
        lane = lax.rem(owners - seq_index + seq_count, seq_count) * capacity + rank
        page_of_lane = jnp.sum(
            jnp.where(lane[None, :] == order[:, None], order[None, :], 0), axis=1
        )
        share = lax.dynamic_slice_in_dim(
            kv_t, lax.rem(mp_index, ratio) * share_width, share_width, 0
        )
        outgoing = reorder(pick_kernel, page_of_lane, share, pages_dev, share_width)
        arrived = [outgoing[:capacity]]
        for d in range(1, seq_count):
            arrived.append(
                lax.ppermute(
                    outgoing[d * capacity:(d + 1) * capacity],
                    "seq",
                    [(i, (i + d) % seq_count) for i in range(seq_count)],
                )
            )

    with jax.named_scope("attention"):
        both = jnp.concatenate([behind, kv_t], axis=1)
        key_rows = both[:head_size].T
        keys = jnp.concatenate([key_rows, key_rows], axis=1)
        vals = jnp.concatenate(
            [both[head_size:], jnp.ones((16, 2 * tok_rows), jnp.bfloat16)], axis=0
        )
        low_row = low[None, :]
        outs, first = [], 0
        for count in CHUNKS:
            att = attend(lows, low_row, q_t, keys, vals, first, count, heads, head_size)
            part = lax.dot_general(
                att, w_output, (((0,), (1,)), ((), ())), preferred_element_type=jnp.float32
            ).astype(jnp.bfloat16)
            outs.append(lax.psum_scatter(part, "mp", scatter_dimension=1, tiled=True))
            first += count
        layer_out = jnp.concatenate(outs, axis=0)

    with jax.named_scope("pages_in"):
        tables = info[:, 1, :pages_dev]
        mine = (tables // pages_dev) == seq_index
        before = jnp.sum(
            jnp.where(order[None, None, :] < order[None, :, None], mine[:, None, :], False).astype(
                jnp.int32
            ),
            axis=2,
        )
        source = jnp.arange(seq_count, dtype=jnp.int32)[:, None]
        shift = lax.rem(seq_index - source + seq_count, seq_count)
        lane_in = jnp.where(mine, shift * capacity + before, 0)
        slot_in = jnp.where(mine, tables % pages_dev, -1)
        lane_of_slot = jnp.sum(
            jnp.where(slot_in[None] == order[:, None, None], lane_in[None], 0), axis=(1, 2)
        )
        kv_cache = reorder(
            place_kernel, lane_of_slot, jnp.concatenate(arrived, axis=0), pages_dev, share_width
        )
    return (layer_out, kv_cache)


def solution(mesh):
    placed = (
        P("seq", None),
        P(),
        P("seq", "mp"),
        P(None, "seq", None),
        P("seq", "mp"),
        P("seq"),
        P("seq"),
    )
    return jax.shard_map(
        body,
        mesh=mesh,
        in_specs=placed,
        out_specs=(P("seq", "mp"), P("seq", "mp", None)),
        check_vma=False,
    )
```

time: 619 us -> 259 us (0.42)
  starting transfers between devices: 207 us -> 62.9 us
  matrix products: 139 us -> 26.1 us
  other arithmetic: 86.4 us -> 13 us
  Pallas kernels: 0 us -> 44.1 us
  loops' own time: 36.9 us -> 0 us
  local copies, waits for them, and re-layouts: 29.8 us -> 7.08 us
  waiting for transfers between devices: 76.4 us -> 62.4 us
    all_to_all x2 -> x0, starting transfers between devices: 205 us -> none  [the longest x1 201 us: body(): lax.all_to_all(labels, 'seq', split_axis=0, concat_axis=0, tiled=True)]
    dot_general x14 -> x6, matrix products: 139 us -> 26.1 us  [the longest x4 12.3 us: body(): lax.dot_general(att, w_output, (((0,), (1,)), ((), ())), preferred_elemen...]
    reduce_sum x5 -> x7, other arithmetic: 62.4 us -> 2.48 us  [the longest x1 0.93 us: body(): jnp.sum(jnp.where(slot_in[None] == order[:, None, None], lane_in[None], 0...]
    ppermute x1 -> x8, starting transfers between devices: 2.27 us -> 62 us  [the longest x7 59.7 us: body(): lax.ppermute(outgoing[d * capacity:(d + 1) * capacity], 'seq', [(i, (i +...]
    pallas_call x0 -> x6, Pallas kernels: none -> 44.1 us  [the longest x4 40.2 us: attend(): pl.pallas_call(functools.partial(attend_kernel, heads, head_size, first,...]
    another operation x11 -> x0, loops' own time: 36.9 us -> none  [the longest x1 21 us: prefix(): return lax.fori_loop(0, count - 1, hop, so_far)]
    all_to_all x2 -> x0, waiting for transfers between devices: 19.1 us -> none  [the longest x1 15.2 us: body(): lax.all_to_all(outgoing, 'seq', split_axis=0, concat_axis=0, tiled=True)]
    all_gather x2, waiting for transfers between devices: 0.02 us -> 13.8 us  [the longest x1 13.7 us: body(): w_output = lax.all_gather(late, 'seq', axis=0, tiled=True)]
  transfers between devices with their start and end apart: 6 -> 14, of which waited for: 4 -> 7; matrix products, arithmetic and copies ran while one was open for 40% -> 13% of each run, Pallas kernels for 0% -> 17%
where the time goes in v1:
time: 259 us; the launch traced here: 260 us
  starting transfers between devices  62.9 us (24%)
  waiting for transfers between devices  62.4 us (24%)
  Pallas kernels  44.1 us (17%)
  blocking collectives  29.9 us (12%)
  matrix products  26.1 us (10%)
  between operations  14.5 us (6%)
  other arithmetic  13 us (5%)
  local copies, waits for them, and re-layouts  7.08 us (3%)
    ppermute x7, starting transfers between devices, body(): lax.ppermute(outgoing[d * capacity:(d + 1) * capacity], 'seq', [(i, (i +...  59.7 us
    reduce_scatter x4, waiting for transfers between devices, body(): outs.append(lax.psum_scatter(part, 'mp', scatter_dimension=1, tiled=True))  42.9 us
    pallas_call x4, Pallas kernels, attend(): pl.pallas_call(functools.partial(attend_kernel, heads, head_size, first,...  40.2 us
    all_gather x1, blocking collectives, body(): w_keyval = lax.all_gather(kv_own, 'seq', axis=0, tiled=True)  18.1 us
    all_gather x1, waiting for transfers between devices, body(): w_output = lax.all_gather(late, 'seq', axis=0, tiled=True)  13.7 us
    dot_general x4, matrix products, body(): lax.dot_general(att, w_output, (((0,), (1,)), ((), ())), preferred_elemen...  12.3 us
    all_gather x1, blocking collectives, body(): info = lax.all_gather(jnp.stack([below, padded]), 'seq')  11.8 us
    dot_general x1, matrix products, body(): lax.dot_general(w_query, normed, (((0,), (1,)), ((), ())), preferred_elem...  8.19 us
  transfers between devices with their start and end apart: 14, of which 7 were waited for; matrix products, arithmetic and copies ran while one was open for 13% of the time, Pallas kernels for 17%

profile of v1, /device:TPU:0, one launch (start us, length us, event | category | flops | bytes accessed | tf_op | source)
XLA Modules:
  0.0 260.0 jit_solution(18292334151958423343)
XLA Ops:
  8.0 5.1 %fusion = f32[2048]{0:T(1024)S(1)} fusion(bf16[2048,2048]{1,0:T(8,128)(2,1)} %param.7), kind=kLoop, calls=%fused_computation.2 | loop fusion | flops 12580864 | bytes 8396800 | tf_op jit(solution)/shard_map/norm/reduce_sum | solution.py:158
  13.1 18.1 %all-gather.1 = bf16[1,2048,128]{2,1,0:T(8,128)(2,1)S(1)} all-gather(bf16[1,256,128]{2,1,0:T(8,128)(2,1)S(1)} %constant_dynamic-slice_fusion), channel_id=3, replica_groups=mesh['seq'=8,'mp'=4] {'seq'}, dimensions={1}, use_global_device_ids=true | all-gather | bytes 589824 | tf_op jit(solution)/shard_map/gathers/all_gather | solution.py:151
  31.2 5.6 %fusion.3 = f32[128,2048]{1,0:T(8,128)S(1)} fusion(bf16[2048,2048]{1,0:T(8,128)(2,1)} %param.7, f32[2048]{0:T(1024)S(1)} %copy-done.13, f32[2048]{0:T(1024)S(1)} %add_rsqrt_fusion, bf16[1,2048,128]{2,1,0:T(8,128)(2,1)S(1)} %all-gather.1), kind=kOutput, calls=%fused_computation.9 | convolution fusion | flops 1090519040 | bytes 9977856 | tf_op jit(solution)/shard_map/keyval/dot_general | solution.py:178
  37.1 11.8 %all-gather.2 = s32[8,2,128]{2,1,0:T(2,128)S(1)} all-gather(s32[1,2,128]{2,1,0:T(2,128)S(1)} %add_bitcast_fusion), channel_id=2, replica_groups=mesh['seq'=8,'mp'=4] {'seq'}, dimensions={0}, use_global_device_ids=true | all-gather | bytes 9216 | tf_op jit(solution)/shard_map/gathers/all_gather | solution.py:149
  49.2 1.2 subtract_convert_fusion.1
  50.4 2.3 collective-permute-start
  52.8 1.4 collective-permute-done
  55.5 8.2 %fusion.5 = f32[512,2048]{1,0:T(8,128)S(1)} fusion(bf16[2048,512]{1,0:T(8,128)(2,1)} %all-gather.6.cloned.1.call-done, bf16[2048,2048]{1,0:T(8,128)(2,1)} %param.7, f32[2048]{0:T(1024)S(1)} %copy-done.13, f32[2048]{0:T(1024)S(1)} %add_rsqrt_fusion), kind=kOutput, calls=%fused_computation.10 | convolution fusion | flops 4311744512 | bytes 14696448 | tf_op jit(solution)/shard_map/queries/dot_general | solution.py:188
  64.6 9.0 %attention.4 = bf16[512,512]{1,0:T(8,128)(2,1)S(1)} custom-call(s32[8]{0:T(128)S(1)} %slice.59.lows, s32[1,2048]{1,0:T(1,128)S(1)} %add_maximum_fusion.low_ref, bf16[512,2048]{1,0:T(8,128)(2,1)S(1)} %bitcast.27, bf16[4096,128]{1,0:T(8,128)(2,1)S(1)} %copy.22.k_ref, bf16[80,4096]{1,0:T(8,128)(2,1)S(1)} %concatenate.27.v_ref), custom_call_target="tpu_custom_call" | custom-call | flops 8589934592 | bytes 6291456 | tf_op jit(solution)/shard_map/attention/pallas_call | solution.py:72
  74.5 13.7 %all-gather.8.cloned.1.call-done = bf16[2048,512]{1,0:T(8,128)(2,1)} async-done(((bf16[256,512]{1,0:T(8,128)(2,1)}), bf16[2048,512]{1,0:T(8,128)(2,1)}) %all-gather.8.cloned.1.call-update) | async-done | bytes 2097168 | tf_op jit(solution)/shard_map/gathers/all_gather | solution.py:154
  88.2 4.4 %convolution_convert_fusion.3 = bf16[512,2048]{1,0:T(8,128)(2,1)} fusion(bf16[512,512]{1,0:T(8,128)(2,1)} %copy-done.5, bf16[2048,512]{1,0:T(8,128)(2,1)} %all-gather.8.cloned.1.call-done), kind=kOutput, calls=%fused_computation.8 | convolution fusion | flops 1074790400 | bytes 4718592 | tf_op jit(solution)/shard_map/attention/dot_general | solution.py:231
  93.0 1.1 copy-done.2
  94.0 9.1 %attention.5 = bf16[512,512]{1,0:T(8,128)(2,1)S(1)} custom-call(s32[8]{0:T(128)S(1)} %slice.59.lows, s32[1,2048]{1,0:T(1,128)S(1)} %add_maximum_fusion.low_ref, bf16[512,2048]{1,0:T(8,128)(2,1)S(1)} %bitcast.28, bf16[4096,128]{1,0:T(8,128)(2,1)S(1)} %copy.22.k_ref, bf16[80,4096]{1,0:T(8,128)(2,1)S(1)} %copy-done.2), custom_call_target="tpu_custom_call" | custom-call | flops 8589934592 | bytes 6291456 | tf_op jit(solution)/shard_map/attention/pallas_call | solution.py:72
  103.1 2.6 %convolution_convert_fusion.2 = bf16[512,2048]{1,0:T(8,128)(2,1)} fusion(bf16[512,512]{1,0:T(8,128)(2,1)S(1)} %attention.5, bf16[2048,512]{1,0:T(8,128)(2,1)S(1)} %copy-done.10), kind=kOutput, calls=%fused_computation.7 | convolution fusion | flops 1074790400 | bytes 4718592 | tf_op jit(solution)/shard_map/attention/dot_general | solution.py:231
  105.8 1.1 copy-done.3
  107.0 9.1 %attention.6 = bf16[512,512]{1,0:T(8,128)(2,1)S(1)} custom-call(s32[8]{0:T(128)S(1)} %slice.59.lows, s32[1,2048]{1,0:T(1,128)S(1)} %add_maximum_fusion.low_ref, bf16[512,2048]{1,0:T(8,128)(2,1)S(1)} %bitcast.29, bf16[4096,128]{1,0:T(8,128)(2,1)S(1)} %copy.22.k_ref, bf16[80,4096]{1,0:T(8,128)(2,1)S(1)} %copy-done.3), custom_call_target="tpu_custom_call" | custom-call | flops 8589934592 | bytes 6291456 | tf_op jit(solution)/shard_map/attention/pallas_call | solution.py:72
  116.0 2.6 %convolution_convert_fusion.1 = bf16[512,2048]{1,0:T(8,128)(2,1)} fusion(bf16[512,512]{1,0:T(8,128)(2,1)S(1)} %attention.6, bf16[2048,512]{1,0:T(8,128)(2,1)S(1)} %copy-done.11), kind=kOutput, calls=%fused_computation.6 | convolution fusion | flops 1074790400 | bytes 4718592 | tf_op jit(solution)/shard_map/attention/dot_general | solution.py:231
  119.0 1.1 copy-done.4
  120.1 13.0 %attention.7 = bf16[512,512]{1,0:T(8,128)(2,1)S(1)} custom-call(s32[8]{0:T(128)S(1)} %slice.59.lows, s32[1,2048]{1,0:T(1,128)S(1)} %add_maximum_fusion.low_ref, bf16[512,2048]{1,0:T(8,128)(2,1)S(1)} %bitcast.30, bf16[4096,128]{1,0:T(8,128)(2,1)S(1)} %copy.22.k_ref, bf16[80,4096]{1,0:T(8,128)(2,1)S(1)} %copy-done.4), custom_call_target="tpu_custom_call" | custom-call | flops 8589934592 | bytes 6291456 | tf_op jit(solution)/shard_map/attention/pallas_call | solution.py:72
  133.2 2.6 %convolution_convert_fusion = bf16[512,2048]{1,0:T(8,128)(2,1)} fusion(bf16[512,512]{1,0:T(8,128)(2,1)S(1)} %attention.7, bf16[2048,512]{1,0:T(8,128)(2,1)S(1)} %copy-done.12), kind=kOutput, calls=%fused_computation.5 | convolution fusion | flops 1074790400 | bytes 4718592 | tf_op jit(solution)/shard_map/attention/dot_general | solution.py:231
  136.8 2.0 pages_out.1
  138.7 1.1 fusion.22
  139.8 24.2 %collective-permute-start.1 = (bf16[2,128,128]{2,1,0:T(8,128)(2,1)S(1)}, bf16[2,128,128]{2,1,0:T(8,128)(2,1)S(1)}, u32[]{:S(2)}, u32[]{:S(2)}) collective-permute-start(bf16[2,128,128]{2,1,0:T(8,128)(2,1)S(1)} %get-tuple-element.20), channel_id=1, source_target_pairs={{0,4},{4,8},{8,12},{12,16},{16,20},{20,24},{24,28},{28,0},{1,5},{5... | collective-permute-start | bytes 196616 | tf_op jit(solution)/shard_map/pages_out/ppermute | solution.py:213
  164.1 29.0 %collective-permute-start.2 = (bf16[2,128,128]{2,1,0:T(8,128)(2,1)S(1)}, bf16[2,128,128]{2,1,0:T(8,128)(2,1)S(1)}, u32[]{:S(2)}, u32[]{:S(2)}) collective-permute-start(bf16[2,128,128]{2,1,0:T(8,128)(2,1)S(1)} %get-tuple-element.19), channel_id=1, source_target_pairs={{0,8},{4,12},{8,16},{12,20},{16,24},{20,28},{24,0},{28,4},{1,9},{5... | collective-permute-start | bytes 196616 | tf_op jit(solution)/shard_map/pages_out/ppermute | solution.py:213
  193.1 3.8 %collective-permute-start.4 = (bf16[2,128,128]{2,1,0:T(8,128)(2,1)S(1)}, bf16[2,128,128]{2,1,0:T(8,128)(2,1)S(1)}, u32[]{:S(2)}, u32[]{:S(2)}) collective-permute-start(bf16[2,128,128]{2,1,0:T(8,128)(2,1)S(1)} %get-tuple-element.17), channel_id=1, source_target_pairs={{0,16},{4,20},{8,24},{12,28},{16,0},{20,4},{24,8},{28,12},{1,17},{... | collective-permute-start | bytes 196616 | tf_op jit(solution)/shard_map/pages_out/ppermute | solution.py:213
  198.1 2.1 collective-permute-start.6
  201.4 1.9 collective-permute-done.4
  203.4 1.2 collective-permute-done.6
  205.4 1.9 pages_in.1
  207.3 4.0 %reduce-scatter.9.cloned.1.call-done = bf16[512,512]{1,0:T(8,128)(2,1)} async-done(((bf16[512,2048]{1,0:T(8,128)(2,1)}), bf16[512,512]{1,0:T(8,128)(2,1)}) %reduce-scatter.9.cloned.1.call-update) | async-done | bytes 524304 | tf_op jit(solution)/shard_map/attention/reduce_scatter | solution.py:234
  211.3 38.9 %reduce-scatter.11.cloned.1.call-done = bf16[512,512]{1,0:T(8,128)(2,1)} async-done(((bf16[512,2048]{1,0:T(8,128)(2,1)}), bf16[512,512]{1,0:T(8,128)(2,1)}) %reduce-scatter.11.cloned.1.call-update) | async-done | bytes 524304 | tf_op jit(solution)/shard_map/attention/reduce_scatter | solution.py:234
  250.2 3.0 %pad_maximum_fusion.1 = bf16[2048,512]{1,0:T(8,128)(2,1)} fusion(bf16[512,512]{1,0:T(8,128)(2,1)} %reduce-scatter.11.cloned.1.call-done, bf16[512,512]{1,0:T(8,128)(2,1)} %reduce-scatter.9.cloned.1.call-done, bf16[512,512]{1,0:T(8,128)(2,1)} %reduce-scatter.7.cloned.1.call-done, bf16[512,512]{1,0:T(8,128)(2,1)} %reduce-scatter.5.cloned.1.call-done), kind=kLoop, calls=%fused_computation.12 | loop fusion | flops 8388608 | bytes 4194304 | tf_op jit(solution)/shard_map/attention/concatenate | solution.py:236
  (86 shorter events, 9.4 us)
Async XLA Ops:
  7.2 5.9 %copy-start = (bf16[4,256,128]{2,1,0:T(8,128)(2,1)S(1)}, bf16[4,256,128]{2,1,0:T(8,128)(2,1)}, u32[]{:S(2)}) copy-start(bf16[4,256,128]{2,1,0:T(8,128)(2,1)} %param.10) | copy-start | bytes 786436
  7.2 47.1 %all-gather.6.cloned.1.call-start = ((), (), s32[]{:S(2)}) async-start(), calls=%async_computation.4 | async-start | bytes 2359296 | tf_op jit(solution)/shard_map/gathers/all_gather | solution.py:152
  7.9 80.3 %all-gather.8.cloned.1.call-start = ((), (), s32[]{:S(2)}) async-start(), calls=%async_computation.5 | async-start | bytes 2359296 | tf_op jit(solution)/shard_map/gathers/all_gather | solution.py:154
  8.0 23.2 %copy-start.13 = (f32[2048]{0:T(1024)S(1)}, f32[2048]{0:T(1024)}, u32[]{:S(2)}) copy-start(f32[2048]{0:T(1024)} %param.8) | copy-start | bytes 24580
  31.2 5.6 %copy-start.9 = (s32[16]{0:T(128)S(1)}, s32[16]{0:T(128)}, u32[]{:S(2)}) copy-start(s32[16]{0:T(128)} %param.13) | copy-start | bytes 196
  31.2 5.6 %copy-start.8 = (s32[2048]{0:T(1024)S(1)}, s32[2048]{0:T(1024)}, u32[]{:S(2)}) copy-start(s32[2048]{0:T(1024)} %param.12) | copy-start | bytes 24580
  50.4 2.4 copy-start.6
  50.4 3.8 %collective-permute-start = (bf16[128,2048]{1,0:T(8,128)(2,1)S(1)}, bf16[128,2048]{1,0:T(8,128)(2,1)S(1)}, u32[]{:S(2)}, u32[]{:S(2)}) collective-permute-start(bf16[128,2048]{1,0:T(8,128)(2,1)S(1)} %pad_maximum_fusion.3.src), channel_id=1, source_target_pairs={{0,4},{4,8},{8,12},{12,16},{16,20},{20,24},{24,28},{1,5},{5,9},{9,... | collective-permute-start | bytes 1572872 | tf_op jit(solution)/shard_map/keyval/ppermute | solution.py:184
  54.3 153.0 %reduce-scatter.5.cloned.1.call-start = ((), (), s32[]{:S(2)}) async-start(), calls=%async_computation.6 | async-start | bytes 2621440 | tf_op jit(solution)/shard_map/attention/reduce_scatter | solution.py:234
  55.5 9.1 %copy-start.1 = (bf16[80,4096]{1,0:T(8,128)(2,1)}, bf16[80,4096]{1,0:T(8,128)(2,1)S(1)}, u32[]{:S(2)}) copy-start(bf16[80,4096]{1,0:T(8,128)(2,1)S(1)} %concatenate.27.v_ref) | copy-start | bytes 1966084
  73.7 0.8 copy-start.5
  92.7 114.6 %reduce-scatter.7.cloned.1.call-start = ((), (), s32[]{:S(2)}) async-start(), calls=%async_computation.7 | async-start | bytes 2621440 | tf_op jit(solution)/shard_map/attention/reduce_scatter | solution.py:234
  92.9 1.1 copy-start.2
  94.0 9.1 %copy-start.10 = (bf16[2048,512]{1,0:T(8,128)(2,1)S(1)}, bf16[2048,512]{1,0:T(8,128)(2,1)}, u32[]{:S(2)}) copy-start(bf16[2048,512]{1,0:T(8,128)(2,1)} %all-gather.8.cloned.1.call-done) | copy-start | bytes 6291460
  105.8 105.5 %reduce-scatter.9.cloned.1.call-start = ((), (), s32[]{:S(2)}) async-start(), calls=%async_computation.8 | async-start | bytes 2621440 | tf_op jit(solution)/shard_map/attention/reduce_scatter | solution.py:234
  105.8 1.1 copy-start.3
  107.0 9.1 %copy-start.11 = (bf16[2048,512]{1,0:T(8,128)(2,1)S(1)}, bf16[2048,512]{1,0:T(8,128)(2,1)}, u32[]{:S(2)}) copy-start(bf16[2048,512]{1,0:T(8,128)(2,1)} %all-gather.8.cloned.1.call-done) | copy-start | bytes 6291460
  118.7 131.5 %reduce-scatter.11.cloned.1.call-start = ((), (), s32[]{:S(2)}) async-start(), calls=%async_computation.9 | async-start | bytes 2621440 | tf_op jit(solution)/shard_map/attention/reduce_scatter | solution.py:234
  119.0 1.1 copy-start.4
  120.1 13.1 %copy-start.12 = (bf16[2048,512]{1,0:T(8,128)(2,1)S(1)}, bf16[2048,512]{1,0:T(8,128)(2,1)}, u32[]{:S(2)}) copy-start(bf16[2048,512]{1,0:T(8,128)(2,1)} %all-gather.8.cloned.1.call-done) | copy-start | bytes 6291460
  139.8 58.3 %collective-permute-start.1 = (bf16[2,128,128]{2,1,0:T(8,128)(2,1)S(1)}, bf16[2,128,128]{2,1,0:T(8,128)(2,1)S(1)}, u32[]{:S(2)}, u32[]{:S(2)}) collective-permute-start(bf16[2,128,128]{2,1,0:T(8,128)(2,1)S(1)} %get-tuple-element.20), channel_id=1, source_target_pairs={{0,4},{4,8},{8,12},{12,16},{16,20},{20,24},{24,28},{28,0},{1,5},{5... | collective-permute-start | bytes 196616 | tf_op jit(solution)/shard_map/pages_out/ppermute | solution.py:213
  164.1 36.1 %collective-permute-start.2 = (bf16[2,128,128]{2,1,0:T(8,128)(2,1)S(1)}, bf16[2,128,128]{2,1,0:T(8,128)(2,1)S(1)}, u32[]{:S(2)}, u32[]{:S(2)}) collective-permute-start(bf16[2,128,128]{2,1,0:T(8,128)(2,1)S(1)} %get-tuple-element.19), channel_id=1, source_target_pairs={{0,8},{4,12},{8,16},{12,20},{16,24},{20,28},{24,0},{28,4},{1,9},{5... | collective-permute-start | bytes 196616 | tf_op jit(solution)/shard_map/pages_out/ppermute | solution.py:213
  193.1 8.4 %collective-permute-start.3 = (bf16[2,128,128]{2,1,0:T(8,128)(2,1)S(1)}, bf16[2,128,128]{2,1,0:T(8,128)(2,1)S(1)}, u32[]{:S(2)}, u32[]{:S(2)}) collective-permute-start(bf16[2,128,128]{2,1,0:T(8,128)(2,1)S(1)} %get-tuple-element.18), channel_id=1, source_target_pairs={{0,12},{4,16},{8,20},{12,24},{16,28},{20,0},{24,4},{28,8},{1,13},{... | collective-permute-start | bytes 196616 | tf_op jit(solution)/shard_map/pages_out/ppermute | solution.py:213
  193.1 10.3 %collective-permute-start.4 = (bf16[2,128,128]{2,1,0:T(8,128)(2,1)S(1)}, bf16[2,128,128]{2,1,0:T(8,128)(2,1)S(1)}, u32[]{:S(2)}, u32[]{:S(2)}) collective-permute-start(bf16[2,128,128]{2,1,0:T(8,128)(2,1)S(1)} %get-tuple-element.17), channel_id=1, source_target_pairs={{0,16},{4,20},{8,24},{12,28},{16,0},{20,4},{24,8},{28,12},{1,17},{... | collective-permute-start | bytes 196616 | tf_op jit(solution)/shard_map/pages_out/ppermute | solution.py:213
  196.8 6.6 %collective-permute-start.5 = (bf16[2,128,128]{2,1,0:T(8,128)(2,1)S(1)}, bf16[2,128,128]{2,1,0:T(8,128)(2,1)S(1)}, u32[]{:S(2)}, u32[]{:S(2)}) collective-permute-start(bf16[2,128,128]{2,1,0:T(8,128)(2,1)S(1)} %get-tuple-element.16), channel_id=1, source_target_pairs={{0,20},{4,24},{8,28},{12,0},{16,4},{20,8},{24,12},{28,16},{1,21},{... | collective-permute-start | bytes 196616 | tf_op jit(solution)/shard_map/pages_out/ppermute | solution.py:213
  198.1 6.5 %collective-permute-start.6 = (bf16[2,128,128]{2,1,0:T(8,128)(2,1)S(1)}, bf16[2,128,128]{2,1,0:T(8,128)(2,1)S(1)}, u32[]{:S(2)}, u32[]{:S(2)}) collective-permute-start(bf16[2,128,128]{2,1,0:T(8,128)(2,1)S(1)} %get-tuple-element.15), channel_id=1, source_target_pairs={{0,24},{4,28},{8,0},{12,4},{16,8},{20,12},{24,16},{28,20},{1,25},{... | collective-permute-start | bytes 196616 | tf_op jit(solution)/shard_map/pages_out/ppermute | solution.py:213
  200.2 4.4 %collective-permute-start.7 = (bf16[2,128,128]{2,1,0:T(8,128)(2,1)S(1)}, bf16[2,128,128]{2,1,0:T(8,128)(2,1)S(1)}, u32[]{:S(2)}, u32[]{:S(2)}) collective-permute-start(bf16[2,128,128]{2,1,0:T(8,128)(2,1)S(1)} %get-tuple-element.14), channel_id=1, source_target_pairs={{0,28},{4,0},{8,4},{12,8},{16,12},{20,16},{24,20},{28,24},{1,29},{... | collective-permute-start | bytes 196616 | tf_op jit(solution)/shard_map/pages_out/ppermute | solution.py:213
  204.6 0.8 copy-start.7
Sparse Core Ops, SparseCore 0:
  9.6 33.9 all-gather.5
  54.5 33.7 all-gather.7
  92.8 42.1 reduce-scatter.4
  138.1 35.1 reduce-scatter.6
  176.1 35.1 reduce-scatter.8
  215.0 35.1 reduce-scatter.10
